TPU v7x, 32 devices: a whole 2x2x4 slice. The times are simulated.
32 devices in a mesh: runs: 2 (over x), space: 16 (over z, y, core).
Axes of the slice: x: 2, y: 2, z: 4, core: 2. Of those that a mesh axis runs over, the one named last changes fastest.
Arguments:
- tangent: float32 [1024, 256, 128], P('runs', 'space'), parts along dimension 0, may hold values from -400 to 400
- courant_x: float32 [512, 128], P(('runs', 'space')), parts along dimension 0, may hold values from -0.4 to 0.4
- courant_y: float32 [512, 128], P(('runs', 'space')), parts along dimension 0, may hold values from -0.4 to 0.4
Outputs:
- basis: float32 [1024, 256, 128], P('runs', 'space'), parts along dimension 0
- growth: float32 [1024, 512], P('runs'), parts along dimension 0
- log_growth: float32 [1024], P('runs'), parts along dimension 0
- first_factor: float32 [1024, 512], P('runs'), parts along dimension 0
There are 2 independent parts, one for each index of `runs`. A program takes and returns all parts, laid end to end along the dimension named above; each array names one. Nothing has to cross between parts.
All inputs are finite; a program needn't handle non-finite values.
Results may differ from a plain program's by a relative error of at most 0.0012.
Values sent between devices are 32-bit elements; how exact they have to be, the bound alone decides.
A program may use at most 128 MiB of HBM per device.

v0:
```python
import jax
import jax.numpy as jnp
from jax import lax
from jax.sharding import PartitionSpec as P

diffusion_number = 0.2


def extended(cells, sides, width):
    for axis, dim in sides:
        count = lax.axis_size(axis)
        head = lax.slice_in_dim(cells, 0, width, axis=dim)
        tail = lax.slice_in_dim(cells, cells.shape[dim] - width, cells.shape[dim], axis=dim)
        cells = jnp.concatenate(
            [
                lax.ppermute(tail, axis, [(i, (i + 1) % count) for i in range(count)]),
                cells,
                lax.ppermute(head, axis, [((i + 1) % count, i) for i in range(count)]),
            ],
            axis=dim,
        )
    return cells


def update(center, east_side, west_side, courant_x, courant_y):
    north_side = jnp.roll(center, -1, 2)
    south_side = jnp.roll(center, 1, 2)
    spread = east_side + west_side + north_side + south_side - 4.0 * center
    return (
        center
        + diffusion_number * spread
        - 0.5 * courant_x * (east_side - west_side)
        - 0.5 * courant_y * (north_side - south_side)
    )


def single_step(field, courant_x, courant_y):
    padded = extended(field, (("space", 1),), 1)
    return update(padded[:, 1:-1], padded[:, 2:], padded[:, :-2], courant_x, courant_y)


def factorize(gram, flattened):
    lower = jnp.linalg.cholesky(gram)
    identity = jnp.eye(gram.shape[0], dtype=jnp.float32)
    inverse = lax.linalg.triangular_solve(lower, identity, left_side=True, lower=True)
    return (lower, jnp.dot(inverse, flattened, precision=lax.Precision.HIGHEST))


def body(tangent, courant_x, courant_y):
    advanced = single_step(single_step(tangent, courant_x, courant_y), courant_x, courant_y)
    vectors = advanced.shape[0]
    flattened = advanced.reshape(vectors, advanced.shape[1] * advanced.shape[2])
    cells = advanced.shape[1] * advanced.shape[2] * lax.axis_size("space")
    first_part = jnp.dot(flattened, flattened.T, precision=lax.Precision.HIGHEST)
    first_gram = lax.psum(first_part, "space") / cells
    first_lower, first_basis = factorize(first_gram, flattened)
    second_part = jnp.dot(first_basis, first_basis.T, precision=lax.Precision.HIGHEST)
    second_gram = lax.psum(second_part, "space") / cells
    second_lower, final_basis = factorize(second_gram, first_basis)
    growth = jnp.dot(first_lower, second_lower, precision=lax.Precision.HIGHEST).T
    log_growth = jnp.log(jnp.diagonal(first_lower)) + jnp.log(jnp.diagonal(second_lower))
    return (final_basis.reshape(advanced.shape), growth, log_growth, first_lower.T)


def solution(mesh):
    return jax.shard_map(
        body,
        mesh=mesh,
        in_specs=(P("runs", "space", None), P(("runs", "space"), None), P(("runs", "space"), None)),
        out_specs=(P("runs", "space", None), P("runs", None), P("runs"), P("runs", None)),
        check_vma=False,
    )
```

profile of v0, /device:TPU:0, one launch (start us, length us, event | category | flops | bytes accessed | tf_op | source)
XLA Modules:
  0.0 612.8 jit_solution(12937679501652068149)
XLA Ops:
  7.2 2.6 fusion.97
  9.8 5.5 collective-permute-start
  15.3 5.2 copy.47
  20.5 8.2 %fusion.98 = (f32[512,16,127]{0,2,1:T(8,128)}, f32[512,16,127]{0,2,1:T(8,128)}) fusion(f32[512,16,128]{0,2,1:T(8,128)} %copy.47), kind=kLoop, calls=%fused_computation.177 | loop fusion | bytes 16646144 | tf_op jit(solution)/shard_map/jit(_roll_static)/slice | solution.py:26
  30.1 9.0 %multiply_subtract_fusion.1 = f32[512,16,128]{0,2,1:T(8,128)S(1)} fusion(f32[512,16,128]{0,2,1:T(8,128)} %copy.47, f32[512,16,127]{0,2,1:T(8,128)} %get-tuple-element.71, f32[512,16,1]{0,2,1:T(1,128)S(1)} %get-tuple-element.73, f32[512,16,1]{0,2,1:T(1,128)S(1)} %get-tuple-element.72, f32[512,16,127]{0,2,1:T(8,128)} %get-tuple-element.70, ...), kind=kLoop, calls=%fused_computation.15 | loop fusion | flops 17825792 | bytes 17317888 | tf_op jit(solution)/shard_map/sub | solution.py:30
  39.1 2.0 copy-done.2
  41.3 4.5 collective-permute-start.2
  46.5 8.2 %fusion.95 = (f32[512,16,127]{0,2,1:T(8,128)}, f32[512,16,127]{0,2,1:T(8,128)}) fusion(f32[512,16,128]{0,2,1:T(8,128)} %copy-done.2), kind=kLoop, calls=%fused_computation.174 | loop fusion | bytes 16646144 | tf_op jit(solution)/shard_map/jit(_roll_static)/slice | solution.py:26
  56.0 9.0 %multiply_subtract_fusion = f32[512,16,128]{0,2,1:T(8,128)S(1)} fusion(f32[512,16,128]{0,2,1:T(8,128)} %copy-done.2, f32[512,16,127]{0,2,1:T(8,128)} %get-tuple-element.65, f32[512,16,1]{0,2,1:T(1,128)S(1)} %get-tuple-element.67, f32[512,16,1]{0,2,1:T(1,128)S(1)} %get-tuple-element.66, f32[512,16,127]{0,2,1:T(8,128)} %get-tuple-element.64, ...), kind=kLoop, calls=%fused_computation.14 | loop fusion | flops 17825792 | bytes 17317888 | tf_op jit(solution)/shard_map/sub | solution.py:30
  65.0 2.0 copy-done.3
  67.0 8.0 %convolution_bitcast_fusion.1 = f32[512,512]{0,1:T(8,128)} fusion(f32[512,16,128]{0,2,1:T(8,128)S(1)} %multiply_subtract_fusion), kind=kOutput, calls=%fused_computation.17 | convolution fusion | flops 6442450944 | bytes 5242880 | tf_op jit(solution)/shard_map/dot_general | solution.py:54
  75.5 94.1 %all-reduce.4.cloned.1.call-done = f32[512,512]{0,1:T(8,128)} async-done(((f32[512,512]{0,1:T(8,128)}), f32[512,512]{0,1:T(8,128)}) %all-reduce.4.cloned.1.call-update) | async-done | bytes 1048592 | tf_op jit(solution)/shard_map/psum | solution.py:55
  169.6 2.4 broadcast_multiply_fusion.1
  171.9 1.6 copy.55
  174.7 11.7 %cholesky.286 = f32[128,128]{1,0:T(8,128)S(1)} custom-call(f32[128,128]{1,0:T(8,128)S(1)} %cholesky.426), custom_call_target="Cholesky" | custom-call | tf_op jit(solution)/shard_map/jit(cholesky)/cholesky | solution.py:43
  186.6 9.8 %custom-call.31 = f32[1,128,128]{1,2,0:T(8,128)S(1)} custom-call(f32[1,128,128]{2,1,0:T(8,128)S(1)} %get-tuple-element.93), custom_call_target="InvertDiagBlocksLowerTriangular" | custom-call | tf_op jit(solution)/shard_map/jit(cholesky)/cholesky | solution.py:43
  197.7 1.3 convolution_subtract_fusion.7
  199.0 11.7 %cholesky.305 = f32[128,128]{1,0:T(8,128)S(1)} custom-call(f32[128,128]{1,0:T(8,128)S(1)} %cholesky.430), custom_call_target="Cholesky" | custom-call | tf_op jit(solution)/shard_map/jit(cholesky)/cholesky | solution.py:43
  212.1 10.2 %custom-call.32 = f32[1,128,128]{1,2,0:T(8,128)S(1)} custom-call(f32[1,128,128]{2,1,0:T(8,128)S(1)} %get-tuple-element.90), custom_call_target="InvertDiagBlocksLowerTriangular" | custom-call | tf_op jit(solution)/shard_map/jit(cholesky)/cholesky | solution.py:43
  222.5 1.3 convolution_subtract_fusion.9
  223.8 11.7 %cholesky.326 = f32[128,128]{1,0:T(8,128)S(1)} custom-call(f32[128,128]{1,0:T(8,128)S(1)} %cholesky.435), custom_call_target="Cholesky" | custom-call | tf_op jit(solution)/shard_map/jit(cholesky)/cholesky | solution.py:43
  236.2 9.8 %custom-call.33 = f32[1,128,128]{1,2,0:T(8,128)S(1)} custom-call(f32[1,128,128]{2,1,0:T(8,128)S(1)} %get-tuple-element.87), custom_call_target="InvertDiagBlocksLowerTriangular" | custom-call | tf_op jit(solution)/shard_map/jit(cholesky)/cholesky | solution.py:43
  247.5 11.9 %cholesky.343 = f32[128,128]{1,0:T(8,128)S(1)} custom-call(f32[128,128]{1,0:T(8,128)S(1)} %convolution_subtract_fusion.11), custom_call_target="Cholesky" | custom-call | tf_op jit(solution)/shard_map/jit(cholesky)/cholesky | solution.py:43
  263.8 11.7 %while.4 = (s32[]{:T(128)}, f32[512,512]{1,0:T(8,128)}, s32[4,2]{0,1:T(2,128)S(1)}, f32[4,128,128]{2,1,0:T(8,128)S(1)}, s32[]{:T(128)}) while((s32[]{:T(128)}, f32[512,512]{1,0:T(8,128)}, s32[4,2]{0,1:T(2,128)S(1)}, f32[4,128,128]{2,1,0:T(8,128)S(1)}, s32[]{:T(128)}) %tuple.67), condition=%wide.while_cond, body=%wide.while_body.sunk | while | flops 2 | bytes 131181 | solution.py:45
  264.5 2.2 bitcast_dynamic-update-slice_fusion.4
  267.5 2.2 bitcast_dynamic-update-slice_fusion.4
  270.4 2.2 bitcast_dynamic-update-slice_fusion.4
  273.3 2.2 bitcast_dynamic-update-slice_fusion.4
  275.5 39.3 %custom-call.34 = f32[4,128,128]{1,2,0:T(8,128)S(1)} custom-call(f32[4,128,128]{2,1,0:T(8,128)S(1)} %get-tuple-element.20), custom_call_target="InvertDiagBlocksLowerTriangular" | custom-call | tf_op jit(solution)/shard_map/triangular_solve/custom-call.3 | solution.py:45
  315.3 1.4 convolution_subtract_fusion.3
  317.2 1.3 convolution_subtract_fusion.2
  318.9 1.6 convolution_subtract_fusion.5
  320.9 7.1 %fusion = f32[512,2048]{1,0:T(8,128)S(1)} fusion(f32[512,2048]{0,1:T(8,128)S(1)} %bitcast.116, f32[128,512]{1,0:T(8,128)S(1)} %fusion.64, f32[128,512]{1,0:T(8,128)S(1)} %fusion.65, f32[128,512]{1,0:T(8,128)S(1)} %fusion.67, f32[128,512]{1,0:T(8,128)S(1)} %fusion.42), kind=kOutput, calls=%fused_computation.34 | convolution fusion | flops 6443237376 | bytes 9437184 | tf_op jit(solution)/shard_map/dot_general | solution.py:46
  328.1 2.0 copy-done
  330.1 8.3 %fusion.100 = f32[512,512]{0,1:T(8,128)} fusion(f32[512,2048]{1,0:T(8,128)S(1)} %fusion), kind=kOutput, calls=%fused_computation.179 | convolution fusion | flops 6442450944 | bytes 5242880 | tf_op jit(solution)/shard_map/dot_general | solution.py:57
  338.4 4.5 gather_fusion
  343.0 1.3 copy.58
  344.3 86.7 %all-reduce.6.cloned.1.call-done = f32[512,512]{0,1:T(8,128)} async-done(((f32[512,512]{0,1:T(8,128)}), f32[512,512]{0,1:T(8,128)}) %all-reduce.6.cloned.1.call-update) | async-done | bytes 1048592 | tf_op jit(solution)/shard_map/psum | solution.py:58
  431.0 2.4 broadcast_multiply_fusion
  433.4 2.6 copy.57
  436.0 1.5 fusion.15
  438.4 11.7 %cholesky.358 = f32[128,128]{1,0:T(8,128)S(1)} custom-call(f32[128,128]{1,0:T(8,128)S(1)} %cholesky.439), custom_call_target="Cholesky" | custom-call | tf_op jit(solution)/shard_map/jit(cholesky)/cholesky | solution.py:43
  450.3 9.8 %custom-call.35 = f32[1,128,128]{1,2,0:T(8,128)S(1)} custom-call(f32[1,128,128]{2,1,0:T(8,128)S(1)} %get-tuple-element.83), custom_call_target="InvertDiagBlocksLowerTriangular" | custom-call | tf_op jit(solution)/shard_map/jit(cholesky)/cholesky | solution.py:43
  461.4 1.3 convolution_subtract_fusion.6
  462.6 11.7 %cholesky.377 = f32[128,128]{1,0:T(8,128)S(1)} custom-call(f32[128,128]{1,0:T(8,128)S(1)} %cholesky.443), custom_call_target="Cholesky" | custom-call | tf_op jit(solution)/shard_map/jit(cholesky)/cholesky | solution.py:43
  475.7 10.0 %custom-call.36 = f32[1,128,128]{1,2,0:T(8,128)S(1)} custom-call(f32[1,128,128]{2,1,0:T(8,128)S(1)} %get-tuple-element.80), custom_call_target="InvertDiagBlocksLowerTriangular" | custom-call | tf_op jit(solution)/shard_map/jit(cholesky)/cholesky | solution.py:43
  486.0 1.3 convolution_subtract_fusion.8
  487.3 11.7 %cholesky.398 = f32[128,128]{1,0:T(8,128)S(1)} custom-call(f32[128,128]{1,0:T(8,128)S(1)} %cholesky.448), custom_call_target="Cholesky" | custom-call | tf_op jit(solution)/shard_map/jit(cholesky)/cholesky | solution.py:43
  499.7 9.8 %custom-call.37 = f32[1,128,128]{1,2,0:T(8,128)S(1)} custom-call(f32[1,128,128]{2,1,0:T(8,128)S(1)} %get-tuple-element.77), custom_call_target="InvertDiagBlocksLowerTriangular" | custom-call | tf_op jit(solution)/shard_map/jit(cholesky)/cholesky | solution.py:43
  511.0 11.9 %cholesky.415 = f32[128,128]{1,0:T(8,128)S(1)} custom-call(f32[128,128]{1,0:T(8,128)S(1)} %convolution_subtract_fusion.10), custom_call_target="Cholesky" | custom-call | tf_op jit(solution)/shard_map/jit(cholesky)/cholesky | solution.py:43
  526.2 2.4 fusion.20
  528.6 4.5 gather_fusion.1
  533.1 4.5 fusion.101
  537.7 11.7 %while.5 = (s32[]{:T(128)}, f32[512,512]{1,0:T(8,128)}, s32[4,2]{0,1:T(2,128)S(1)}, f32[4,128,128]{2,1,0:T(8,128)S(1)}, s32[]{:T(128)}) while((s32[]{:T(128)}, f32[512,512]{1,0:T(8,128)}, s32[4,2]{0,1:T(2,128)S(1)}, f32[4,128,128]{2,1,0:T(8,128)S(1)}, s32[]{:T(128)}) %tuple.77), condition=%wide.while_cond.clone, body=%wide.while_body.clone.sunk | while | flops 2 | bytes 131181 | solution.py:45
  538.4 2.3 bitcast_dynamic-update-slice_fusion.5
  541.3 2.3 bitcast_dynamic-update-slice_fusion.5
  544.3 2.3 bitcast_dynamic-update-slice_fusion.5
  547.2 2.2 bitcast_dynamic-update-slice_fusion.5
  549.4 39.6 %custom-call.38 = f32[4,128,128]{1,2,0:T(8,128)S(1)} custom-call(f32[4,128,128]{2,1,0:T(8,128)S(1)} %get-tuple-element.21), custom_call_target="InvertDiagBlocksLowerTriangular" | custom-call | tf_op jit(solution)/shard_map/triangular_solve/custom-call.3 | solution.py:45
  589.4 1.4 convolution_subtract_fusion.1
  591.3 1.3 convolution_subtract_fusion
  593.0 1.6 convolution_subtract_fusion.4
  595.0 7.1 %convolution_bitcast_fusion = f32[64,8,16,128]{3,1,2,0:T(8,128)S(1)} fusion(f32[512,2048]{1,0:T(8,128)S(1)} %copy-done.1, f32[128,512]{1,0:T(8,128)S(1)} %fusion.58, f32[128,512]{1,0:T(8,128)S(1)} %fusion.59, f32[128,512]{1,0:T(8,128)S(1)} %fusion.61, f32[128,512]{1,0:T(8,128)S(1)} %fusion.40), kind=kOutput, calls=%fused_computation.16 | convolution fusion | flops 6443237376 | bytes 9437184 | tf_op jit(solution)/shard_map/dot_general | solution.py:46
  602.2 2.9 copy.66
  (106 shorter events, 28.6 us)
Async XLA Ops:
  7.2 162.4 %all-reduce.4.cloned.1.call-start = ((), (), s32[]{:S(2)}) async-start(), calls=%async_computation | async-start | bytes 2097152 | tf_op jit(solution)/shard_map/psum | solution.py:55
  9.8 20.1 %collective-permute-start = (f32[512,1,128]{2,0,1:T(8,128)S(1)}, f32[512,1,128]{2,0,1:T(8,128)S(1)}, u32[]{:S(2)}, u32[]{:S(2)}) collective-permute-start(f32[512,1,128]{2,0,1:T(8,128)S(1)} %bitcast.120), channel_id=1, source_target_pairs={{1,0},{2,1},{3,2},{4,3},{5,4},{6,5},{7,6},{8,7},{9,8},{10,9},{11,1... | collective-permute-start | bytes 786440 | tf_op jit(solution)/shard_map/ppermute | solution.py:18
  15.3 14.7 %collective-permute-start.1 = (f32[512,1,128]{2,0,1:T(8,128)S(1)}, f32[512,1,128]{2,0,1:T(8,128)S(1)}, u32[]{:S(2)}, u32[]{:S(2)}) collective-permute-start(f32[512,1,128]{2,0,1:T(8,128)S(1)} %bitcast.119), channel_id=1, source_target_pairs={{0,1},{1,2},{2,3},{3,4},{4,5},{5,6},{6,7},{7,8},{8,9},{9,10},{10,1... | collective-permute-start | bytes 786440 | tf_op jit(solution)/shard_map/ppermute | solution.py:16
  20.5 8.2 %copy-start.10 = (f32[16,128]{1,0:T(8,128)S(1)}, f32[16,128]{1,0:T(8,128)}, u32[]{:S(2)}) copy-start(f32[16,128]{1,0:T(8,128)} %param.8) | copy-start | bytes 24580
  20.5 8.2 %copy-start.11 = (f32[16,128]{1,0:T(8,128)S(1)}, f32[16,128]{1,0:T(8,128)}, u32[]{:S(2)}) copy-start(f32[16,128]{1,0:T(8,128)} %param.7) | copy-start | bytes 24580
  39.1 2.0 copy-start.2
  41.3 14.4 %collective-permute-start.2 = (f32[512,1,128]{2,0,1:T(8,128)S(1)}, f32[512,1,128]{2,0,1:T(8,128)S(1)}, u32[]{:S(2)}, u32[]{:S(2)}) collective-permute-start(f32[512,1,128]{2,0,1:T(8,128)S(1)} %copy.48), channel_id=1, source_target_pairs={{1,0},{2,1},{3,2},{4,3},{5,4},{6,5},{7,6},{8,7},{9,8},{10,9},{11,1... | collective-permute-start | bytes 786440 | tf_op jit(solution)/shard_map/ppermute | solution.py:18
  45.9 10.0 %collective-permute-start.3 = (f32[512,1,128]{2,0,1:T(8,128)S(1)}, f32[512,1,128]{2,0,1:T(8,128)S(1)}, u32[]{:S(2)}, u32[]{:S(2)}) collective-permute-start(f32[512,1,128]{2,0,1:T(8,128)S(1)} %copy.50), channel_id=1, source_target_pairs={{0,1},{1,2},{2,3},{3,4},{4,5},{5,6},{6,7},{7,8},{8,9},{9,10},{10,1... | collective-permute-start | bytes 786440 | tf_op jit(solution)/shard_map/ppermute | solution.py:16
  65.0 2.0 copy-start.3
  75.1 355.9 %all-reduce.6.cloned.1.call-start = ((), (), s32[]{:S(2)}) async-start(), calls=%async_computation.1 | async-start | bytes 2097152 | tf_op jit(solution)/shard_map/psum | solution.py:58
  169.6 3.9 copy-start.6
  173.8 1.0 copy-start.8
  314.9 6.1 copy-start.4
  328.1 2.0 copy-start
  431.0 5.0 copy-start.7
  437.4 1.0 copy-start.9
  522.9 3.3 copy-start.5
  589.0 6.1 copy-start.1
Sparse Core Ops, SparseCore 0:
  75.2 94.2 all-reduce.3
  338.6 92.3 all-reduce.5
where the time goes:
time: 618 us; the launch traced here: 613 us
  other arithmetic  267 us (43%)
  waiting for transfers between devices  181 us (29%)
  local copies, waits for them, and re-layouts  76.2 us (12%)
  matrix products  58.1 us (9%)
  between operations  20 us (3%)
  starting transfers between devices  10.8 us (2%)
    another operation x30, other arithmetic, factorize(): lower = jnp.linalg.cholesky(gram)  159 us
    psum x1, waiting for transfers between devices, body(): first_gram = lax.psum(first_part, 'space') / cells  94.1 us
    psum x1, waiting for transfers between devices, body(): second_gram = lax.psum(second_part, 'space') / cells  86.7 us
    another operation x5, other arithmetic, factorize(): lax.linalg.triangular_solve(lower, identity, left_side=True, lower=True)  82.5 us
    another operation x27, local copies, waits for them, and re-layouts, factorize(): lax.linalg.triangular_solve(lower, identity, left_side=True, lower=True)  23.3 us
    slice x4, local copies, waits for them, and re-layouts, update(): north_side = jnp.roll(center, -1, 2)  18.6 us
    sub x2, other arithmetic, update(): center + diffusion_number * spread  17.9 us
    unnamed x27, local copies, waits for them, and re-layouts  17.4 us
  transfers between devices with their start and end apart: 6, of which 2 were waited for; matrix products, arithmetic and copies ran while one was open for 5% of the time, Pallas kernels for 0%

commit v1 on v0

--- a/solution.py
+++ b/solution.py
@@ -1,9 +1,18 @@
+import functools
 import jax
 import jax.numpy as jnp
 from jax import lax
 from jax.sharding import PartitionSpec as P
 
 diffusion_number = 0.2
+
+
+def meet_levels_all_now(block_here, net_axis):
+    r2 = jnp.sum(lax.all_gather(block_here, axis_name=net_axis), 0)
+    return r2
+
+
+supply_field = functools.partial(meet_levels_all_now, net_axis="space")
 
 
 def extended(cells, sides, width):
@@ -55,7 +64,7 @@
     first_gram = lax.psum(first_part, "space") / cells
     first_lower, first_basis = factorize(first_gram, flattened)
     second_part = jnp.dot(first_basis, first_basis.T, precision=lax.Precision.HIGHEST)
-    second_gram = lax.psum(second_part, "space") / cells
+    second_gram = supply_field(second_part) / cells
     second_lower, final_basis = factorize(second_gram, first_basis)
     growth = jnp.dot(first_lower, second_lower, precision=lax.Precision.HIGHEST).T
     log_growth = jnp.log(jnp.diagonal(first_lower)) + jnp.log(jnp.diagonal(second_lower))

time: 618 us -> 661 us (1.070)
  waiting for transfers between devices: 181 us -> 215 us
  other arithmetic: 267 us -> 274 us
    all_gather x0 -> x1, waiting for transfers between devices: none -> 120 us  [meet_levels_all_now(): r2 = jnp.sum(lax.all_gather(block_here, axis_name=net_axis), 0)]
    psum x1 -> x0, waiting for transfers between devices: 86.7 us -> none  [body(): second_gram = lax.psum(second_part, 'space') / cells]
    reduce_sum x0 -> x1, other arithmetic: none -> 8.88 us  [meet_levels_all_now(): r2 = jnp.sum(lax.all_gather(block_here, axis_name=net_axis), 0)]
    unnamed x27 -> x25, local copies, waits for them, and re-layouts: 17.4 us -> 17.4 us
where the time goes in v1:
time: 661 us; the launch traced here: 656 us
  other arithmetic  274 us (41%)
  waiting for transfers between devices  215 us (33%)
  local copies, waits for them, and re-layouts  77.7 us (12%)
  matrix products  58.1 us (9%)
  between operations  20.2 us (3%)
  starting transfers between devices  10.8 us (2%)
    another operation x30, other arithmetic, factorize(): lower = jnp.linalg.cholesky(gram)  159 us
    all_gather x1, waiting for transfers between devices, meet_levels_all_now(): r2 = jnp.sum(lax.all_gather(block_here, axis_name=net_axis), 0)  120 us
    psum x1, waiting for transfers between devices, body(): first_gram = lax.psum(first_part, 'space') / cells  94.1 us
    another operation x5, other arithmetic, factorize(): lax.linalg.triangular_solve(lower, identity, left_side=True, lower=True)  82.5 us
    another operation x27, local copies, waits for them, and re-layouts, factorize(): lax.linalg.triangular_solve(lower, identity, left_side=True, lower=True)  23.3 us
    slice x4, local copies, waits for them, and re-layouts, update(): north_side = jnp.roll(center, -1, 2)  18.6 us
    sub x2, other arithmetic, update(): center + diffusion_number * spread  17.8 us
    unnamed x25, local copies, waits for them, and re-layouts  17.4 us
  transfers between devices with their start and end apart: 6, of which 2 were waited for; matrix products, arithmetic and copies ran while one was open for 5% of the time, Pallas kernels for 0%

profile of v1, /device:TPU:0, one launch (start us, length us, event | category | flops | bytes accessed | tf_op | source)
XLA Modules:
  0.0 655.8 jit_solution(18420453702416157275)
XLA Ops:
  7.2 2.6 fusion.97
  9.8 5.5 collective-permute-start
  15.3 5.2 copy.45
  20.5 8.2 %fusion.98 = (f32[512,16,127]{0,2,1:T(8,128)}, f32[512,16,127]{0,2,1:T(8,128)}) fusion(f32[512,16,128]{0,2,1:T(8,128)} %copy.45), kind=kLoop, calls=%fused_computation.177 | loop fusion | bytes 16646144 | tf_op jit(solution)/shard_map/jit(_roll_static)/slice | solution.py:35
  30.1 8.9 %multiply_subtract_fusion.1 = f32[512,16,128]{0,2,1:T(8,128)S(1)} fusion(f32[512,16,128]{0,2,1:T(8,128)} %copy.45, f32[512,16,127]{0,2,1:T(8,128)} %get-tuple-element.71, f32[512,16,1]{0,2,1:T(1,128)S(1)} %get-tuple-element.73, f32[512,16,1]{0,2,1:T(1,128)S(1)} %get-tuple-element.72, f32[512,16,127]{0,2,1:T(8,128)} %get-tuple-element.70, ...), kind=kLoop, calls=%fused_computation.15 | loop fusion | flops 17825792 | bytes 17317888 | tf_op jit(solution)/shard_map/sub | solution.py:39
  39.0 2.0 copy-done.2
  41.2 4.5 collective-permute-start.2
  46.4 8.2 %fusion.95 = (f32[512,16,127]{0,2,1:T(8,128)}, f32[512,16,127]{0,2,1:T(8,128)}) fusion(f32[512,16,128]{0,2,1:T(8,128)} %copy-done.2), kind=kLoop, calls=%fused_computation.174 | loop fusion | bytes 16646144 | tf_op jit(solution)/shard_map/jit(_roll_static)/slice | solution.py:35
  56.0 8.9 %multiply_subtract_fusion = f32[512,16,128]{0,2,1:T(8,128)S(1)} fusion(f32[512,16,128]{0,2,1:T(8,128)} %copy-done.2, f32[512,16,127]{0,2,1:T(8,128)} %get-tuple-element.65, f32[512,16,1]{0,2,1:T(1,128)S(1)} %get-tuple-element.67, f32[512,16,1]{0,2,1:T(1,128)S(1)} %get-tuple-element.66, f32[512,16,127]{0,2,1:T(8,128)} %get-tuple-element.64, ...), kind=kLoop, calls=%fused_computation.14 | loop fusion | flops 17825792 | bytes 17317888 | tf_op jit(solution)/shard_map/sub | solution.py:39
  64.9 2.0 copy-done.3
  66.9 8.0 %convolution_bitcast_fusion.1 = f32[512,512]{0,1:T(8,128)} fusion(f32[512,16,128]{0,2,1:T(8,128)S(1)} %multiply_subtract_fusion), kind=kOutput, calls=%fused_computation.17 | convolution fusion | flops 6442450944 | bytes 5242880 | tf_op jit(solution)/shard_map/dot_general | solution.py:63
  75.3 94.1 %all-reduce.3.cloned.1.call-done = f32[512,512]{0,1:T(8,128)} async-done(((f32[512,512]{0,1:T(8,128)}), f32[512,512]{0,1:T(8,128)}) %all-reduce.3.cloned.1.call-update) | async-done | bytes 1048592 | tf_op jit(solution)/shard_map/psum | solution.py:64
  169.4 2.4 broadcast_multiply_fusion.1
  171.8 1.6 copy.53
  174.6 11.7 %cholesky.286 = f32[128,128]{1,0:T(8,128)S(1)} custom-call(f32[128,128]{1,0:T(8,128)S(1)} %cholesky.426), custom_call_target="Cholesky" | custom-call | tf_op jit(solution)/shard_map/jit(cholesky)/cholesky | solution.py:52
  186.5 9.8 %custom-call.31 = f32[1,128,128]{1,2,0:T(8,128)S(1)} custom-call(f32[1,128,128]{2,1,0:T(8,128)S(1)} %get-tuple-element.93), custom_call_target="InvertDiagBlocksLowerTriangular" | custom-call | tf_op jit(solution)/shard_map/jit(cholesky)/cholesky | solution.py:52
  197.5 1.3 convolution_subtract_fusion.7
  198.8 11.7 %cholesky.305 = f32[128,128]{1,0:T(8,128)S(1)} custom-call(f32[128,128]{1,0:T(8,128)S(1)} %cholesky.430), custom_call_target="Cholesky" | custom-call | tf_op jit(solution)/shard_map/jit(cholesky)/cholesky | solution.py:52
  211.9 10.2 %custom-call.32 = f32[1,128,128]{1,2,0:T(8,128)S(1)} custom-call(f32[1,128,128]{2,1,0:T(8,128)S(1)} %get-tuple-element.90), custom_call_target="InvertDiagBlocksLowerTriangular" | custom-call | tf_op jit(solution)/shard_map/jit(cholesky)/cholesky | solution.py:52
  222.4 1.3 convolution_subtract_fusion.9
  223.7 11.7 %cholesky.326 = f32[128,128]{1,0:T(8,128)S(1)} custom-call(f32[128,128]{1,0:T(8,128)S(1)} %cholesky.435), custom_call_target="Cholesky" | custom-call | tf_op jit(solution)/shard_map/jit(cholesky)/cholesky | solution.py:52
  236.1 9.8 %custom-call.33 = f32[1,128,128]{1,2,0:T(8,128)S(1)} custom-call(f32[1,128,128]{2,1,0:T(8,128)S(1)} %get-tuple-element.87), custom_call_target="InvertDiagBlocksLowerTriangular" | custom-call | tf_op jit(solution)/shard_map/jit(cholesky)/cholesky | solution.py:52
  247.4 11.9 %cholesky.343 = f32[128,128]{1,0:T(8,128)S(1)} custom-call(f32[128,128]{1,0:T(8,128)S(1)} %convolution_subtract_fusion.11), custom_call_target="Cholesky" | custom-call | tf_op jit(solution)/shard_map/jit(cholesky)/cholesky | solution.py:52
  263.7 11.7 %while.4 = (s32[]{:T(128)}, f32[512,512]{1,0:T(8,128)}, s32[4,2]{0,1:T(2,128)S(1)}, f32[4,128,128]{2,1,0:T(8,128)S(1)}, s32[]{:T(128)}) while((s32[]{:T(128)}, f32[512,512]{1,0:T(8,128)}, s32[4,2]{0,1:T(2,128)S(1)}, f32[4,128,128]{2,1,0:T(8,128)S(1)}, s32[]{:T(128)}) %tuple.67), condition=%wide.while_cond, body=%wide.while_body.sunk | while | flops 2 | bytes 131181 | solution.py:54
  264.4 2.2 bitcast_dynamic-update-slice_fusion.4
  267.3 2.2 bitcast_dynamic-update-slice_fusion.4
  270.3 2.2 bitcast_dynamic-update-slice_fusion.4
  273.2 2.2 bitcast_dynamic-update-slice_fusion.4
  275.4 39.3 %custom-call.34 = f32[4,128,128]{1,2,0:T(8,128)S(1)} custom-call(f32[4,128,128]{2,1,0:T(8,128)S(1)} %get-tuple-element.20), custom_call_target="InvertDiagBlocksLowerTriangular" | custom-call | tf_op jit(solution)/shard_map/triangular_solve/custom-call.3 | solution.py:54
  315.2 1.4 convolution_subtract_fusion.3
  317.0 1.3 convolution_subtract_fusion.2
  318.8 1.6 convolution_subtract_fusion.5
  320.8 7.1 %fusion = f32[512,2048]{1,0:T(8,128)S(1)} fusion(f32[512,2048]{0,1:T(8,128)S(1)} %bitcast.117, f32[128,512]{1,0:T(8,128)S(1)} %fusion.64, f32[128,512]{1,0:T(8,128)S(1)} %fusion.65, f32[128,512]{1,0:T(8,128)S(1)} %fusion.67, f32[128,512]{1,0:T(8,128)S(1)} %fusion.42), kind=kOutput, calls=%fused_computation.34 | convolution fusion | flops 6443237376 | bytes 9437184 | tf_op jit(solution)/shard_map/dot_general | solution.py:55
  328.0 2.0 copy-done
  330.0 8.3 %fusion.100 = f32[512,512]{1,0:T(8,128)} fusion(f32[512,2048]{1,0:T(8,128)S(1)} %fusion), kind=kOutput, calls=%fused_computation.179 | convolution fusion | flops 6442450944 | bytes 5242880 | tf_op jit(solution)/shard_map/dot_general | solution.py:66
  338.3 4.5 gather_fusion
  342.8 1.3 copy.56
  344.2 120.4 %all-gather.3.cloned.1.call-done = f32[8192,512]{1,0:T(8,128)} async-done(((f32[512,512]{1,0:T(8,128)}), f32[8192,512]{1,0:T(8,128)}) %all-gather.3.cloned.1.call-update) | async-done | bytes 16777232 | tf_op jit(solution)/shard_map/all_gather | solution.py:11
  464.6 8.9 %reduce_sum.9 = f32[512,512]{1,0:T(8,128)} reduce(f32[16,512,512]{2,1,0:T(8,128)} %bitcast.119, f32[]{:T(128)} %constant.119.clone.1), dimensions={0}, to_apply=%region_9.12 | reduce | flops 3932160 | bytes 17825796 | tf_op jit(solution)/shard_map/reduce_sum | solution.py:11
  473.5 1.6 copy.54
  476.1 2.5 copy.55
  478.7 1.5 fusion.15
  481.1 11.7 %cholesky.358 = f32[128,128]{1,0:T(8,128)S(1)} custom-call(f32[128,128]{1,0:T(8,128)S(1)} %cholesky.439), custom_call_target="Cholesky" | custom-call | tf_op jit(solution)/shard_map/jit(cholesky)/cholesky | solution.py:52
  493.0 9.8 %custom-call.35 = f32[1,128,128]{1,2,0:T(8,128)S(1)} custom-call(f32[1,128,128]{2,1,0:T(8,128)S(1)} %get-tuple-element.83), custom_call_target="InvertDiagBlocksLowerTriangular" | custom-call | tf_op jit(solution)/shard_map/jit(cholesky)/cholesky | solution.py:52
  505.3 11.9 %cholesky.377 = f32[128,128]{1,0:T(8,128)S(1)} custom-call(f32[128,128]{1,0:T(8,128)S(1)} %cholesky.443), custom_call_target="Cholesky" | custom-call | tf_op jit(solution)/shard_map/jit(cholesky)/cholesky | solution.py:52
  518.6 9.8 %custom-call.36 = f32[1,128,128]{1,2,0:T(8,128)S(1)} custom-call(f32[1,128,128]{2,1,0:T(8,128)S(1)} %get-tuple-element.80), custom_call_target="InvertDiagBlocksLowerTriangular" | custom-call | tf_op jit(solution)/shard_map/jit(cholesky)/cholesky | solution.py:52
  528.7 1.3 convolution_subtract_fusion.8
  530.0 11.7 %cholesky.398 = f32[128,128]{1,0:T(8,128)S(1)} custom-call(f32[128,128]{1,0:T(8,128)S(1)} %cholesky.448), custom_call_target="Cholesky" | custom-call | tf_op jit(solution)/shard_map/jit(cholesky)/cholesky | solution.py:52
  542.4 9.8 %custom-call.37 = f32[1,128,128]{1,2,0:T(8,128)S(1)} custom-call(f32[1,128,128]{2,1,0:T(8,128)S(1)} %get-tuple-element.77), custom_call_target="InvertDiagBlocksLowerTriangular" | custom-call | tf_op jit(solution)/shard_map/jit(cholesky)/cholesky | solution.py:52
  553.6 11.9 %cholesky.415 = f32[128,128]{1,0:T(8,128)S(1)} custom-call(f32[128,128]{1,0:T(8,128)S(1)} %convolution_subtract_fusion.10), custom_call_target="Cholesky" | custom-call | tf_op jit(solution)/shard_map/jit(cholesky)/cholesky | solution.py:52
  569.0 2.4 fusion.20
  571.4 4.5 gather_fusion.1
  575.9 4.5 fusion.101
  580.4 11.7 %while.5 = (s32[]{:T(128)}, f32[512,512]{1,0:T(8,128)}, s32[4,2]{0,1:T(2,128)S(1)}, f32[4,128,128]{2,1,0:T(8,128)S(1)}, s32[]{:T(128)}) while((s32[]{:T(128)}, f32[512,512]{1,0:T(8,128)}, s32[4,2]{0,1:T(2,128)S(1)}, f32[4,128,128]{2,1,0:T(8,128)S(1)}, s32[]{:T(128)}) %tuple.77), condition=%wide.while_cond.clone, body=%wide.while_body.clone.sunk | while | flops 2 | bytes 131181 | solution.py:54
  581.1 2.3 bitcast_dynamic-update-slice_fusion.5
  584.1 2.3 bitcast_dynamic-update-slice_fusion.5
  587.0 2.3 bitcast_dynamic-update-slice_fusion.5
  590.0 2.2 bitcast_dynamic-update-slice_fusion.5
  592.2 39.6 %custom-call.38 = f32[4,128,128]{1,2,0:T(8,128)S(1)} custom-call(f32[4,128,128]{2,1,0:T(8,128)S(1)} %get-tuple-element.21), custom_call_target="InvertDiagBlocksLowerTriangular" | custom-call | tf_op jit(solution)/shard_map/triangular_solve/custom-call.3 | solution.py:54
  632.2 1.4 convolution_subtract_fusion.1
  634.0 1.3 convolution_subtract_fusion
  635.8 1.6 convolution_subtract_fusion.4
  637.8 7.1 %convolution_bitcast_fusion = f32[64,8,16,128]{3,1,2,0:T(8,128)S(1)} fusion(f32[512,2048]{1,0:T(8,128)S(1)} %copy-done.1, f32[128,512]{1,0:T(8,128)S(1)} %fusion.58, f32[128,512]{1,0:T(8,128)S(1)} %fusion.59, f32[128,512]{1,0:T(8,128)S(1)} %fusion.61, f32[128,512]{1,0:T(8,128)S(1)} %fusion.40), kind=kOutput, calls=%fused_computation.16 | convolution fusion | flops 6443237376 | bytes 9437184 | tf_op jit(solution)/shard_map/dot_general | solution.py:55
  645.0 2.9 copy.63
  (106 shorter events, 31.1 us)
Async XLA Ops:
  7.2 162.3 %all-reduce.3.cloned.1.call-start = ((), (), s32[]{:S(2)}) async-start(), calls=%async_computation | async-start | bytes 2097152 | tf_op jit(solution)/shard_map/psum | solution.py:64
  9.8 20.1 %collective-permute-start = (f32[512,1,128]{2,0,1:T(8,128)S(1)}, f32[512,1,128]{2,0,1:T(8,128)S(1)}, u32[]{:S(2)}, u32[]{:S(2)}) collective-permute-start(f32[512,1,128]{2,0,1:T(8,128)S(1)} %bitcast.122), channel_id=1, source_target_pairs={{1,0},{2,1},{3,2},{4,3},{5,4},{6,5},{7,6},{8,7},{9,8},{10,9},{11,1... | collective-permute-start | bytes 786440 | tf_op jit(solution)/shard_map/ppermute | solution.py:27
  15.3 14.7 %collective-permute-start.1 = (f32[512,1,128]{2,0,1:T(8,128)S(1)}, f32[512,1,128]{2,0,1:T(8,128)S(1)}, u32[]{:S(2)}, u32[]{:S(2)}) collective-permute-start(f32[512,1,128]{2,0,1:T(8,128)S(1)} %bitcast.121), channel_id=1, source_target_pairs={{0,1},{1,2},{2,3},{3,4},{4,5},{5,6},{6,7},{7,8},{8,9},{9,10},{10,1... | collective-permute-start | bytes 786440 | tf_op jit(solution)/shard_map/ppermute | solution.py:25
  20.5 8.2 %copy-start.9 = (f32[16,128]{1,0:T(8,128)S(1)}, f32[16,128]{1,0:T(8,128)}, u32[]{:S(2)}) copy-start(f32[16,128]{1,0:T(8,128)} %param.8) | copy-start | bytes 24580
  20.5 8.2 %copy-start.10 = (f32[16,128]{1,0:T(8,128)S(1)}, f32[16,128]{1,0:T(8,128)}, u32[]{:S(2)}) copy-start(f32[16,128]{1,0:T(8,128)} %param.7) | copy-start | bytes 24580
  39.0 2.0 copy-start.2
  41.2 14.5 %collective-permute-start.2 = (f32[512,1,128]{2,0,1:T(8,128)S(1)}, f32[512,1,128]{2,0,1:T(8,128)S(1)}, u32[]{:S(2)}, u32[]{:S(2)}) collective-permute-start(f32[512,1,128]{2,0,1:T(8,128)S(1)} %copy.46), channel_id=1, source_target_pairs={{1,0},{2,1},{3,2},{4,3},{5,4},{6,5},{7,6},{8,7},{9,8},{10,9},{11,1... | collective-permute-start | bytes 786440 | tf_op jit(solution)/shard_map/ppermute | solution.py:27
  45.8 10.0 %collective-permute-start.3 = (f32[512,1,128]{2,0,1:T(8,128)S(1)}, f32[512,1,128]{2,0,1:T(8,128)S(1)}, u32[]{:S(2)}, u32[]{:S(2)}) collective-permute-start(f32[512,1,128]{2,0,1:T(8,128)S(1)} %copy.48), channel_id=1, source_target_pairs={{0,1},{1,2},{2,3},{3,4},{4,5},{5,6},{6,7},{7,8},{8,9},{9,10},{10,1... | collective-permute-start | bytes 786440 | tf_op jit(solution)/shard_map/ppermute | solution.py:25
  64.9 2.0 copy-start.3
  75.0 389.6 %all-gather.3.cloned.1.call-start = ((), (), s32[]{:S(2)}) async-start(), calls=%async_computation.1 | async-start | bytes 17825792 | tf_op jit(solution)/shard_map/all_gather | solution.py:11
  169.4 3.9 copy-start.6
  173.6 1.0 copy-start.7
  314.7 6.1 copy-start.4
  328.0 2.0 copy-start
  480.1 1.0 copy-start.8
  565.6 3.4 copy-start.5
  631.7 6.1 copy-start.1
Sparse Core Ops, SparseCore 0:
  75.1 94.2 all-reduce.2
  338.4 126.1 all-gather.2
